TPU v7x, 256 devices: a whole 4x4x8 slice. The times are simulated.
256 devices in a mesh: band: 64 (over z, y, x_hi), grid: 4 (over x_lo, core).
Axes of the slice: x: 4 (x_hi: 2, x_lo: 2; x = x_hi * 2 + x_lo), y: 4, z: 8, core: 2. Of those that a mesh axis runs over, the one named last changes fastest.
Arguments:
- orbitals: float32 [64, 64, 4096], P('band', 'grid')
- counts: int32 [64], P('band'), may hold values from 1 to 3, 144 in all
- partners: int32 [64, 3], P('band'), may hold values from 0 to 63, as said below
Outputs:
- applied: float32 [64, 64, 4096], P('band', 'grid')
Inputs may be any that keep to these rules, and one draw needn't show every extreme that they name: `counts`: some band has exactly 3 listed partners. `partners`: for band i held by band device m = i, every entry j (used or not) satisfies 0 < (j - i) mod 64 and (j - m) mod 64 < 4; the entries of one band are distinct.
All inputs are finite; a program needn't handle non-finite values. No bound on the sum of `counts` on one device may be relied on, other than what follows from the above.
Results may differ from a plain program's by a relative error of at most 0.0001.
Values sent between devices are 32-bit elements; how exact they have to be, the bound alone decides.
A program may use at most 64 MiB of HBM per device.

v0:
```python
import functools
import math

import jax
import jax.numpy as jnp
import ml_dtypes
import numpy as np
from jax import lax
from jax.experimental import pallas as pl
from jax.experimental.pallas import tpu as pltpu
from jax.sharding import PartitionSpec as P

MESH = pl.DeviceIdType.MESH
F32, BF16 = jnp.float32, jnp.bfloat16
NG = 64
PLANE = NG * NG
WIDE = PLANE + 128
A, B, C, D, E = range(5)
PAIRS = ((B, C, 1), (B, D, 2), (C, D, 1), (A, D, 3), (B, E, 3), (C, E, 2))
PER = 2
CHUNKS = len(PAIRS) // PER


def basis():
    n = np.arange(NG)
    rows = [np.full(NG, 1 / 8)]
    rows += [np.cos(2 * np.pi * k * n / NG) * math.sqrt(2) / 8 for k in range(1, 32)]
    rows += [np.cos(np.pi * n) / 8]
    rows += [np.sin(2 * np.pi * k * n / NG) * math.sqrt(2) / 8 for k in range(1, 32)]
    return np.stack(rows)


def halves(m):
    high = m.astype(np.float32).astype(ml_dtypes.bfloat16)
    low = (m - high.astype(np.float64)).astype(np.float32).astype(ml_dtypes.bfloat16)
    return high, low


def left(m):
    high, low = halves(m)
    return np.concatenate([high, high, low], 1)


def right(m):
    high, low = halves(m)
    return np.concatenate([np.concatenate([high, low], 1), np.concatenate([high, np.zeros_like(low)], 1)], 0)


def tables():
    r = basis()
    zero = np.zeros_like(r)
    z_fwd = np.block([[r.T, zero], [zero, r.T]])
    z_inv = np.block([[r, zero], [zero, r]])
    t = {(e, q): r[32 * e : 32 * e + 32, q::2] for e in range(2) for q in range(2)}
    y_fwd = np.block([[t[0, 0], t[0, 1]], [t[1, 1], t[1, 0]]])
    y_inv = np.block([[t[0, 0].T, t[1, 0].T], [t[1, 1].T, t[0, 1].T]])
    return (
        np.stack([right(z_fwd), right(z_inv)]),
        np.stack([left(y_fwd), left(y_inv), left(r), left(r.T)]),
    )


def split(x):
    high = x.astype(BF16)
    return high, (x - high.astype(F32)).astype(BF16)


def dot(a, b):
    return lax.dot_general(a, b, (((1,), (0,)), ((), ())), preferred_element_type=F32)


def from_left(matrix, x):
    high, low = split(x)
    return dot(matrix, jnp.concatenate([high, low, high], 0))


def from_right(x, matrix):
    high, low = split(x)
    both = dot(jnp.concatenate([high, low], 1), matrix)
    return both[:, :128] + both[:, 128:]


def along_y(ref, field, matrix):
    parts = []
    for f in range(PER):
        for x in range(8):
            parts.append(ref[field + f, pl.ds(x, 32, stride=8), :])
    both = jnp.concatenate(parts, 1)
    other = jnp.concatenate([jnp.concatenate([v[:, 64:], v[:, :64]], 1) for v in parts], 1)
    out = from_left(matrix, jnp.concatenate([both, other], 0))
    lane = lax.broadcasted_iota(jnp.int32, (32, 128), 1)
    res = []
    for n in range(8 * PER):
        piece = out[:, 128 * n : 128 * (n + 1)]
        res.append(jnp.where(lane < 64, piece[:32], piece[32:]))
    return res


def freq_sq(index):
    f = jnp.where(index <= 32, index, index - 32).astype(F32) * F32(2 * math.pi / NG)
    return f * f


def kernel(
    orb, counts, partners, wz_ref, wl_ref, out_ref,
    band, other, s1, s2, got, back, s3, s4, acc, ret, lam,
    local_sem, f_send, f_recv, t1_send, t1_recv, t2_send, t2_recv, r_send, r_recv,
):
    m = lax.axis_index("band")
    g = lax.axis_index("grid")
    p, h = m // 2, m % 2
    me = 2 * g + h
    n_bands = 64

    def at(dp, hh):
        return ((2 * p + 2 * dp + n_bands) % n_bands + hh, g)

    def peer(slot):
        return (2 * p + slot % 2, slot // 2)

    def remote(src, dst, send, recv, device):
        return pltpu.make_async_remote_copy(
            src_ref=src, dst_ref=dst, send_sem=send, recv_sem=recv, device_id=device, device_id_type=MESH
        )

    own = pltpu.make_async_copy(orb.at[pl.ds(8 * h, 8), :], band.at[1 + h, :, pl.ds(0, PLANE)], local_sem.at[0])
    rest = pltpu.make_async_copy(orb.at[pl.ds(8 * (1 - h), 8), :], other.at[:, pl.ds(0, PLANE)], local_sem.at[1])
    own.start()
    rest.start()

    barrier = pltpu.get_barrier_semaphore()
    for k in range(1, 8):
        pl.semaphore_signal(barrier, inc=1, device_id=peer(me ^ k), device_id_type=MESH)
    for dp in (-1, 1):
        for hh in range(2):
            pl.semaphore_signal(barrier, inc=1, device_id=at(dp, hh), device_id_type=MESH)

    row = lax.broadcasted_iota(jnp.int32, (8, 128), 0)
    tile = jnp.zeros((8, 128), F32)
    for d in range(1, 4):
        listed = jnp.float32(0.0)
        for k in range(3):
            hit = ((partners[0, k] - m + n_bands) % n_bands == d) & (counts[0] > k)
            listed = listed + jnp.where(hit, jnp.float32(1.0), jnp.float32(0.0))
        tile = jnp.where(row == d - 1, listed, tile)
    band[1 + h, :, PLANE:] = tile
    other[:, PLANE:] = tile

    kx = freq_sq(lax.broadcasted_iota(jnp.int32, (NG, 128), 0))
    lane = lax.broadcasted_iota(jnp.int32, (NG, 128), 1)
    kz = freq_sq(lane % 64)
    for i in range(4):
        ky = freq_sq(4 * me + i + jnp.where(lane < 64, 0, 32))
        total = kx + ky + kz
        some = total > 0
        lam[:, 128 * i : 128 * (i + 1)] = jnp.where(some, F32(4 * math.pi) / jnp.where(some, total, 1.0), 0.0)

    own.wait()
    rest.wait()
    pl.semaphore_wait(barrier, 11)

    mine = band.at[1 + h]
    fetches = [
        remote(other, band.at[1 + h], f_send.at[0], f_recv.at[1 + h], at(0, 1 - h)),
        remote(other, band.at[3 + h], f_send.at[1], f_recv.at[3 + h], at(-1, 1 - h)),
        remote(mine, band.at[3 + h], f_send.at[2], f_recv.at[3 + h], at(-1, h)),
    ]
    upward = [
        remote(other, band.at[A], f_send.at[3], f_recv.at[A], at(1, 0)),
        remote(mine, band.at[A], f_send.at[4], f_recv.at[A], at(1, 1)),
    ]
    for copy in fetches:
        copy.start()

    @pl.when(h == 1)
    def _():
        for copy in upward:
            copy.start()

    def fetched(slot):
        remote(other, band.at[slot], f_send.at[0], f_recv.at[slot], at(0, 0)).wait_recv()

    fetched(2 - h)
    ready = {B, C}
    sent1 = []
    order = (1, 3, 5, 7, 4, 6, 2)
    for c in range(CHUNKS):
        f0 = PER * c
        for f in range(f0, f0 + PER):
            low, high, d = PAIRS[f]
            for slot in (low, high):
                if slot not in ready:
                    fetched(slot)
                    ready.add(slot)
            alive = jnp.broadcast_to(band[low, d - 1 : d, PLANE:], (8, 128))
            pieces = []
            for j in range(32):
                cut = slice(128 * j, 128 * (j + 1))
                pieces.append(band[low, :, cut] * band[high, :, cut] * alive)
            s1[f] = from_right(jnp.concatenate(pieces, 0), wz_ref[0])
        res = along_y(s1, f0, wl_ref[0])
        for f in range(PER):
            for x in range(8):
                s2[f0 + f, pl.ds(x, 32, stride=8), :] = res[8 * f + x]
        for k in order:
            to = me ^ k
            copy = remote(
                s2.at[pl.ds(f0, PER), pl.ds(pl.multiple_of(32 * to, 32), 32)],
                got.at[me, pl.ds(f0, PER)],
                t1_send.at[c, k], t1_recv.at[c, k], peer(to),
            )
            copy.start()
            sent1.append(copy)
        got[me, f0 : f0 + PER] = s2[f0 : f0 + PER, pl.ds(pl.multiple_of(32 * me, 32), 32)]

    sent2 = []
    for c in range(CHUNKS):
        f0 = PER * c
        for k in order:
            remote(
                s2.at[pl.ds(f0, PER), pl.ds(0, 32)], got.at[me ^ k, pl.ds(f0, PER)],
                t1_send.at[c, k], t1_recv.at[c, k], peer(me ^ k),
            ).wait_recv()
        columns = []
        for f in range(f0, f0 + PER):
            for i in range(4):
                columns.append(jnp.concatenate([got[s, f, 8 * i : 8 * i + 8, :] for s in range(8)], 0))
        wave = from_left(wl_ref[2], jnp.concatenate(columns, 1))
        wave = wave * jnp.concatenate([lam[...]] * PER, 1)
        wave = from_left(wl_ref[3], wave)
        for f in range(PER):
            for i in range(4):
                n = 4 * f + i
                for s in range(8):
                    back[s, f0 + f, 8 * i : 8 * i + 8, :] = wave[8 * s : 8 * s + 8, 128 * n : 128 * (n + 1)]
        for k in order:
            to = me ^ k
            copy = remote(
                back.at[to, pl.ds(f0, PER)],
                s3.at[pl.ds(f0, PER), pl.ds(pl.multiple_of(32 * me, 32), 32)],
                t2_send.at[c, k], t2_recv.at[c, k], peer(to),
            )
            copy.start()
            sent2.append(copy)
        s3[f0 : f0 + PER, pl.ds(pl.multiple_of(32 * me, 32), 32)] = back[me, f0 : f0 + PER]

    gives = {
        D: remote(acc.at[D], ret.at[1 + h], r_send.at[0], r_recv.at[1 + h], at(1, 0)),
        A: remote(acc.at[A], ret.at[3 + h], r_send.at[1], r_recv.at[3 + h], at(-1, 1)),
        E: remote(acc.at[E], ret.at[1 + h], r_send.at[2], r_recv.at[1 + h], at(1, 1)),
        C: remote(acc.at[2 - h], ret.at[0], r_send.at[3], r_recv.at[0], at(0, 1 - h)),
    }
    begun = set()
    last = {slot: max(f for f, pair in enumerate(PAIRS) if slot in pair[:2]) for slot in range(5)}
    for c in range(CHUNKS):
        f0 = PER * c
        for k in order:
            remote(
                back.at[0, pl.ds(f0, PER)], s3.at[pl.ds(f0, PER), pl.ds(pl.multiple_of(32 * (me ^ k), 32), 32)],
                t2_send.at[c, k], t2_recv.at[c, k], peer(me ^ k),
            ).wait_recv()
        res = along_y(s3, f0, wl_ref[1])
        for f in range(PER):
            for x in range(8):
                s4[f0 + f, pl.ds(x, 32, stride=8), :] = res[8 * f + x]
        for f in range(f0, f0 + PER):
            low, high, _ = PAIRS[f]
            potential = from_right(s4[f], wz_ref[1])
            for j in range(32):
                cut = slice(128 * j, 128 * (j + 1))
                v = potential[8 * j : 8 * j + 8]
                for to, by in ((low, high), (high, low)):
                    term = v * band[by, :, cut]
                    acc[to, :, cut] = acc[to, :, cut] + term if to in begun else term
            begun |= {low, high}
        for slot, copy in gives.items():
            if f0 <= last[slot] < f0 + PER:
                copy.start()

    def returned(slot):
        remote(acc.at[0], ret.at[slot], r_send.at[0], r_recv.at[slot], at(0, 0)).wait_recv()

    returned(1)
    returned(2)

    @pl.when(h == 1)
    def _():
        returned(3)
        returned(4)
        ret[1] = ret[1] + ret[3]
        ret[2] = ret[2] + ret[4]

    out_ref[pl.ds(pl.multiple_of(8 * h, 8), 8), :] = acc[1 + h] + ret[1 + h]
    returned(0)
    out_ref[pl.ds(pl.multiple_of(8 * (1 - h), 8), 8), :] = ret[0] + ret[2 - h]

    for copy in fetches + sent1 + sent2 + list(gives.values()):
        copy.wait_send()

    @pl.when(h == 1)
    def _():
        for copy in upward:
            copy.wait_send()


def shards(orbitals, counts, partners):
    wz, wl = tables()
    fields = len(PAIRS)
    vmem = pl.BlockSpec(memory_space=pltpu.VMEM)
    smem = pl.BlockSpec(memory_space=pltpu.SMEM)
    dma = pltpu.SemaphoreType.DMA
    applied = pl.pallas_call(
        kernel,
        out_shape=jax.ShapeDtypeStruct((16, PLANE), F32),
        in_specs=[pl.BlockSpec(memory_space=pl.ANY), smem, smem, vmem, vmem],
        out_specs=vmem,
        scratch_shapes=[
            pltpu.VMEM((5, 8, WIDE), F32),
            pltpu.VMEM((8, WIDE), F32),
            pltpu.VMEM((fields, 256, 128), F32),
            pltpu.VMEM((fields, 256, 128), F32),
            pltpu.VMEM((8, fields, 32, 128), F32),
            pltpu.VMEM((8, fields, 32, 128), F32),
            pltpu.VMEM((fields, 256, 128), F32),
            pltpu.VMEM((fields, 256, 128), F32),
            pltpu.VMEM((5, 8, PLANE), F32),
            pltpu.VMEM((5, 8, PLANE), F32),
            pltpu.VMEM((NG, 512), F32),
            dma((2,)),
            dma((5,)),
            dma((5,)),
            dma((CHUNKS, 8)),
            dma((CHUNKS, 8)),
            dma((CHUNKS, 8)),
            dma((CHUNKS, 8)),
            dma((4,)),
            dma((5,)),
        ],
        compiler_params=pltpu.CompilerParams(
            collective_id=0, has_side_effects=True, vmem_limit_bytes=32 * 1024 * 1024
        ),
        cost_estimate=pl.CostEstimate(flops=500_000_000, bytes_accessed=1 << 20, transcendentals=0),
    )(orbitals.reshape(16, PLANE), counts, partners, jnp.asarray(wz), jnp.asarray(wl))
    return applied.reshape(1, 16, PLANE)


def solution(mesh):
    in_specs = (P("band", "grid", None), P("band"), P("band", None))
    out_specs = P("band", "grid", None)
    return jax.shard_map(shards, mesh=mesh, in_specs=in_specs, out_specs=out_specs, check_vma=False)
```

profile of v0, /device:TPU:1, one launch (start us, length us, event | category | flops | bytes accessed | tf_op | source)
XLA Modules:
  0.0 54.1 jit_solution(5034468149908440602)
XLA Ops:
  0.7 0.0 copy-start.1
  0.7 0.6 %copy-done.1 = s32[1,3]{1,0:T(1,128)S(1)} copy-done((s32[1,3]{1,0:T(1,128)S(1)}, s32[1,3]{1,0:T(1,128)}, u32[]{:S(2)}) %copy-start.1) | copy-done | bytes 36
  1.3 0.0 copy-start
  1.3 0.9 %copy-done = f32[1,16,4096]{2,1,0:T(8,128)S(1)} copy-done((f32[1,16,4096]{2,1,0:T(8,128)S(1)}, f32[1,16,4096]{2,1,0:T(8,128)}, u32[]{:S(2)}) %copy-start) | copy-done | bytes 262168
  2.3 0.0 copy-start.2
  2.3 0.9 %copy-done.2 = bf16[2,256,256]{2,1,0:T(8,128)(2,1)S(1)} copy-done((bf16[2,256,256]{2,1,0:T(8,128)(2,1)S(1)}, bf16[2,256,256]{2,1,0:T(8,128)(2,1)}, u32[]{:S(2)}) %copy-start.2) | copy-done | bytes 262168
  3.2 0.0 copy-start.3
  3.2 0.9 %copy-done.3 = bf16[4,64,192]{2,1,0:T(8,128)(2,1)S(1)} copy-done((bf16[4,64,192]{2,1,0:T(8,128)(2,1)S(1)}, bf16[4,64,192]{2,1,0:T(8,128)(2,1)}, u32[]{:S(2)}) %copy-start.3) | copy-done | bytes 98328
  4.1 49.3 %shard_map.55 = f32[16,4096]{1,0:T(8,128)S(1)} custom-call(f32[16,4096]{1,0:T(8,128)S(1)} %bitcast.3, s32[1]{0:T(128)S(6)} %copy.7.counts, s32[1,3]{1,0:T(1,128)S(1)} %copy-done.1, bf16[2,256,256]{2,1,0:T(8,128)(2,1)S(1)} %copy-done.2, bf16[4,64,192]{2,1,0:T(8,128)(2,1)S(1)} %copy-done.3), custom_call_target="tpu_custom_call" | custom-call | flops 500000000 | bytes 1048576 | tf_op jit(solution)/shard_map/pallas_call | solution.py:312
  53.4 0.7 %copy.8 = f32[1,16,4096]{2,1,0:T(8,128)} copy(f32[1,16,4096]{2,1,0:T(8,128)S(1)} %bitcast.2) | data formatting | bytes 524288
Async XLA Ops:
  0.7 0.7 %copy-start.1 = (s32[1,3]{1,0:T(1,128)S(1)}, s32[1,3]{1,0:T(1,128)}, u32[]{:S(2)}) copy-start(s32[1,3]{1,0:T(1,128)} %partners.1) | copy-start | bytes 40
  1.3 0.9 %copy-start = (f32[1,16,4096]{2,1,0:T(8,128)S(1)}, f32[1,16,4096]{2,1,0:T(8,128)}, u32[]{:S(2)}) copy-start(f32[1,16,4096]{2,1,0:T(8,128)} %param.5) | copy-start | bytes 786436
  2.3 0.9 %copy-start.2 = (bf16[2,256,256]{2,1,0:T(8,128)(2,1)S(1)}, bf16[2,256,256]{2,1,0:T(8,128)(2,1)}, u32[]{:S(2)}) copy-start(bf16[2,256,256]{2,1,0:T(8,128)(2,1)} %constant.4.clone.wz_ref) | copy-start | bytes 786436
  3.2 0.9 %copy-start.3 = (bf16[4,64,192]{2,1,0:T(8,128)(2,1)S(1)}, bf16[4,64,192]{2,1,0:T(8,128)(2,1)}, u32[]{:S(2)}) copy-start(bf16[4,64,192]{2,1,0:T(8,128)(2,1)} %constant.5.clone.wl_ref) | copy-start | bytes 294916
where the time goes:
time: 55.1 us; the launch traced here: 54.1 us
  Pallas kernels  49.3 us (89%)
  local copies, waits for them, and re-layouts  4.16 us (8%)
  between operations  0.67 us (1%)
    pallas_call x1, Pallas kernels, shards(): pl.pallas_call(kernel, out_shape=jax.ShapeDtypeStruct((16, PLANE), F32),...  49.3 us
    unnamed x9, local copies, waits for them, and re-layouts  4.16 us

commit v1 on v0

v1 whole, which is shorter than its diff:
```python
import functools
import math

import jax
import jax.numpy as jnp
import ml_dtypes
import numpy as np
from jax import lax
from jax.experimental import pallas as pl
from jax.experimental.pallas import tpu as pltpu
from jax.sharding import PartitionSpec as P

MESH = pl.DeviceIdType.MESH
F32, BF16 = jnp.float32, jnp.bfloat16
NG = 64
PLANE = NG * NG
B, C, D, E, F = range(5)
PAIRS = ((D, E, 1), (C, F, 3), (C, D, 1), (C, E, 2), (B, D, 2), (B, E, 3))
RUNS = ((0, 1), (1, 2), (3, 2), (5, 1))
PLAN = (("f", 0), ("f", 1), ("f", 2), ("x", 0), ("f", 3), ("x", 1), ("x", 2), ("x", 3), ("i", 0), ("i", 1), ("i", 2), ("i", 3))


def basis():
    n = np.arange(NG)
    rows = [np.full(NG, 1 / 8)]
    rows += [np.cos(2 * np.pi * k * n / NG) * math.sqrt(2) / 8 for k in range(1, 32)]
    rows += [np.cos(np.pi * n) / 8]
    rows += [np.sin(2 * np.pi * k * n / NG) * math.sqrt(2) / 8 for k in range(1, 32)]
    return np.stack(rows)


def halves(m):
    high = m.astype(np.float32).astype(ml_dtypes.bfloat16)
    low = (m - high.astype(np.float64)).astype(np.float32).astype(ml_dtypes.bfloat16)
    return high, low


def left(m):
    high, low = halves(m)
    return np.concatenate([high, high, low], 1)


def right(m):
    high, low = halves(m)
    return np.concatenate([np.concatenate([high, low], 1), np.concatenate([high, np.zeros_like(low)], 1)], 0)


def tables():
    r = basis()
    zero = np.zeros_like(r)
    z_fwd = np.block([[r.T, zero], [zero, r.T]])
    z_inv = np.block([[r, zero], [zero, r]])
    t = {(e, q): r[32 * e : 32 * e + 32, q::2] for e in range(2) for q in range(2)}
    y_fwd = np.block([[t[0, 0], t[0, 1]], [t[1, 1], t[1, 0]]])
    y_inv = np.block([[t[0, 0].T, t[1, 0].T], [t[1, 1].T, t[0, 1].T]])
    return (
        np.stack([right(z_fwd), right(z_inv)]),
        np.stack([left(y_fwd), left(y_inv), left(r), left(r.T)]),
    )


def split(x):
    high = x.astype(BF16)
    return high, (x - high.astype(F32)).astype(BF16)


def dot(a, b):
    return lax.dot_general(a, b, (((1,), (0,)), ((), ())), preferred_element_type=F32)


def from_left(matrix, x):
    high, low = split(x)
    return dot(matrix, jnp.concatenate([high, low, high], 0))


def from_right(x, matrix):
    high, low = split(x)
    both = dot(jnp.concatenate([high, low], 1), matrix)
    return both[:, :128] + both[:, 128:]


def along_y(ref, first, count, matrix):
    parts = []
    for f in range(first, first + count):
        for x in range(8):
            parts.append(ref[f, pl.ds(x, 32, stride=8), :])
    both = jnp.concatenate(parts, 1)
    other = jnp.concatenate([jnp.concatenate([v[:, 64:], v[:, :64]], 1) for v in parts], 1)
    out = from_left(matrix, jnp.concatenate([both, other], 0))
    lane = lax.broadcasted_iota(jnp.int32, (32, 128), 1)
    res = []
    for n in range(8 * count):
        piece = out[:, 128 * n : 128 * (n + 1)]
        res.append(jnp.where(lane < 64, piece[:32], piece[32:]))
    return res


def freq_sq(index):
    f = jnp.where(index <= 32, index, index - 32).astype(F32) * F32(2 * math.pi / NG)
    return f * f


def kernel(
    orb, counts_in, partners_in, wz_in, wl_in, out_ref,
    counts, partners, wz_ref, wl_ref, band, listed, s1, s2, got, back, s3, s4, acc, ret, lam,
    local_sem, hello, f_send, f_recv, a_send, a_recv, t1_send, t1_recv, t2_send, t2_recv, r_send, r_recv,
):
    m = lax.axis_index("band")
    g = lax.axis_index("grid")
    p, h = m // 2, m % 2
    me = 2 * g + h
    n_bands = 64

    def at(dp, hh):
        return ((2 * p + 2 * dp + n_bands) % n_bands + hh, g)

    def peer(slot):
        return (2 * p + slot % 2, slot // 2)

    def remote(src, dst, send, recv, device):
        return pltpu.make_async_remote_copy(
            src_ref=src, dst_ref=dst, send_sem=send, recv_sem=recv, device_id=device, device_id_type=MESH
        )

    barrier = pltpu.get_barrier_semaphore()
    for device in [at(-1, 0), at(-1, 1)] + [peer(me ^ k) for k in (1, 2, 4, 6)]:
        pl.semaphore_signal(barrier, inc=1, device_id=device, device_id_type=MESH)

    def rows(half):
        return pl.ds(pl.multiple_of(8 * half, 8), 8)

    mine, rest = orb.at[rows(h)], orb.at[rows(1 - h)]
    local = [
        pltpu.make_async_copy(src, dst, local_sem.at[n])
        for n, (src, dst) in enumerate(
            (
                (counts_in, counts), (partners_in, partners), (mine, band.at[D + h]),
                (wz_in, wz_ref), (wl_in, wl_ref),
            )
        )
    ]
    for copy in local:
        copy.start()

    pl.semaphore_wait(barrier, 6)

    def fetch(src, slot, n, device):
        return remote(src, band.at[slot], f_send.at[n], f_recv.at[slot], device)

    def fetched(slot):
        fetch(rest, slot, 0, at(0, 1 - h)).wait_recv()

    def tell(slot, n, device):
        return remote(listed.at[D + h], listed.at[slot], a_send.at[n], a_recv.at[slot], device)

    sent = [
        fetch(rest, D + h, 0, at(0, 1 - h)),
        fetch(mine, B + h, 1, at(1, h)),
    ]
    for copy in sent:
        copy.start()
    for hh in range(2):
        pl.semaphore_signal(hello, inc=1, device_id=at(1, hh), device_id_type=MESH)

    local[0].wait()
    local[1].wait()
    row = lax.broadcasted_iota(jnp.int32, (8, 128), 0)
    tile = jnp.zeros((8, 128), F32)
    for d in range(1, 4):
        weight = jnp.float32(0.0)
        for k in range(3):
            hit = ((partners[0, k] - m + n_bands) % n_bands == d) & (counts[0] > k)
            weight = weight + jnp.where(hit, jnp.float32(1.0), jnp.float32(0.0))
        tile = jnp.where(row == d - 1, weight, tile)
    listed[D + h] = tile
    told = [tell(D + h, 0, at(0, 1 - h)), tell(B + h, 1, at(1, h))]
    for copy in told:
        copy.start()
    sent += told

    kx = freq_sq(lax.broadcasted_iota(jnp.int32, (NG, 128), 0))
    lane = lax.broadcasted_iota(jnp.int32, (NG, 128), 1)
    kz = freq_sq(lane % 64)
    for i in range(4):
        ky = freq_sq(4 * me + i + jnp.where(lane < 64, 0, 32))
        total = kx + ky + kz
        some = total > 0
        lam[:, 128 * i : 128 * (i + 1)] = jnp.where(some, F32(4 * math.pi) / jnp.where(some, total, 1.0), 0.0)

    for copy in local[2:]:
        copy.wait()
    fetched(E - h)
    tell(E - h, 0, at(0, 1 - h)).wait_recv()
    on = [
        fetch(band.at[E - h], C - h, 2, at(1, h)),
        remote(listed.at[E - h], listed.at[C - h], a_send.at[2], a_recv.at[C - h], at(1, h)),
        fetch(band.at[D], F, 3, at(-1, h)),
    ]
    on[0].start()
    on[1].start()
    pl.semaphore_wait(hello, 2)
    on[2].start()
    sent += on
    ready = {D, E}
    order = (1, 3, 5, 7, 4, 6, 2)
    mine_32 = pl.ds(pl.multiple_of(32 * me, 32), 32)

    def forward(c):
        f0, count = RUNS[c]
        run = pl.ds(f0, count)
        for f in range(f0, f0 + count):
            low, high, d = PAIRS[f]
            for slot in (low, high):
                if slot not in ready:
                    fetched(slot)
                    if slot != F:
                        tell(slot, 0, at(0, 1 - h)).wait_recv()
                    ready.add(slot)
            alive = jnp.broadcast_to(listed[low, d - 1 : d, :], (8, 128))
            pieces = []
            for j in range(32):
                cut = slice(128 * j, 128 * (j + 1))
                pieces.append(band[low, :, cut] * band[high, :, cut] * alive)
            s1[f] = from_right(jnp.concatenate(pieces, 0), wz_ref[0])
        res = along_y(s1, f0, count, wl_ref[0])
        for n, piece in enumerate(res):
            s2[f0 + n // 8, pl.ds(n % 8, 32, stride=8), :] = piece
        for k in order:
            to = me ^ k
            copy = remote(
                s2.at[run, pl.ds(pl.multiple_of(32 * to, 32), 32)], got.at[me, run],
                t1_send.at[c, k], t1_recv.at[c, k], peer(to),
            )
            copy.start()
            sent.append(copy)
        got[me, f0 : f0 + count] = s2[f0 : f0 + count, mine_32]

    def across(c):
        f0, count = RUNS[c]
        run = pl.ds(f0, count)
        for k in order:
            remote(
                s2.at[run, pl.ds(0, 32)], got.at[me ^ k, run], t1_send.at[c, k], t1_recv.at[c, k], peer(me ^ k)
            ).wait_recv()
        columns = []
        for f in range(f0, f0 + count):
            for i in range(4):
                columns.append(jnp.concatenate([got[s, f, 8 * i : 8 * i + 8, :] for s in range(8)], 0))
        wave = from_left(wl_ref[2], jnp.concatenate(columns, 1))
        wave = wave * jnp.concatenate([lam[...]] * count, 1)
        wave = from_left(wl_ref[3], wave)
        for f in range(count):
            for i in range(4):
                n = 4 * f + i
                for s in range(8):
                    back[s, f0 + f, 8 * i : 8 * i + 8, :] = wave[8 * s : 8 * s + 8, 128 * n : 128 * (n + 1)]
        for k in order:
            to = me ^ k
            copy = remote(back.at[to, run], s3.at[run, mine_32], t2_send.at[c, k], t2_recv.at[c, k], peer(to))
            copy.start()
            sent.append(copy)
        s3[f0 : f0 + count, mine_32] = back[me, f0 : f0 + count]

    def give(slot, to, n, device):
        return remote(acc.at[slot], ret.at[to], r_send.at[n], r_recv.at[to], device)

    gives = {
        B: give(B, 1 + h, 0, at(-1, 0)),
        C: give(C, 3, 1, at(-1, h)),
        F: give(F, 4, 2, at(1, h)),
    }
    swap = give(E - h, 0, 3, at(0, 1 - h))
    begun = set()
    left_of = {slot: sum(slot in pair[:2] for pair in PAIRS) for slot in gives}

    def inverse(c):
        f0, count = RUNS[c]
        run = pl.ds(f0, count)
        for k in order:
            remote(
                back.at[0, run], s3.at[run, pl.ds(pl.multiple_of(32 * (me ^ k), 32), 32)],
                t2_send.at[c, k], t2_recv.at[c, k], peer(me ^ k),
            ).wait_recv()
        res = along_y(s3, f0, count, wl_ref[1])
        for n, piece in enumerate(res):
            s4[f0 + n // 8, pl.ds(n % 8, 32, stride=8), :] = piece
        for f in range(f0, f0 + count):
            low, high, _ = PAIRS[f]
            potential = from_right(s4[f], wz_ref[1])
            for j in range(32):
                cut = slice(128 * j, 128 * (j + 1))
                v = potential[8 * j : 8 * j + 8]
                for to, by in ((low, high), (high, low)):
                    term = v * band[by, :, cut]
                    acc[to, :, cut] = acc[to, :, cut] + term if to in begun else term
            begun.update((low, high))
            for slot in (low, high):
                if slot in gives:
                    left_of[slot] -= 1
                    if not left_of[slot]:
                        gives[slot].start()

    steps = {"f": forward, "x": across, "i": inverse}
    for step, c in PLAN:
        steps[step](c)

    def returned(slot):
        give(B, slot, 0, at(-1, 0)).wait_recv()

    returned(4)
    returned(3)
    acc[D] = acc[D] + ret[4]
    acc[E] = acc[E] + ret[3]
    swap.start()

    @pl.when(h == 0)
    def _():
        returned(1)
        returned(2)
        out_ref[0:8, :] = acc[D] + ret[1]
        returned(0)
        out_ref[8:16, :] = ret[0] + ret[2]

    @pl.when(h == 1)
    def _():
        out_ref[8:16, :] = acc[E]
        returned(0)
        out_ref[0:8, :] = ret[0]

    for copy in sent + list(gives.values()) + [swap]:
        copy.wait_send()


def shards(orbitals, counts, partners):
    wz, wl = tables()
    fields = len(PAIRS)
    vmem = pl.BlockSpec(memory_space=pltpu.VMEM)
    hbm = pl.BlockSpec(memory_space=pl.ANY)
    dma = pltpu.SemaphoreType.DMA

    def held(x):
        return pltpu.with_memory_space_constraint(x, pltpu.HBM)

    applied = pl.pallas_call(
        kernel,
        out_shape=jax.ShapeDtypeStruct((16, PLANE), F32),
        in_specs=[hbm] * 5,
        out_specs=vmem,
        scratch_shapes=[
            pltpu.SMEM((1,), jnp.int32),
            pltpu.SMEM((1, 3), jnp.int32),
            pltpu.VMEM(wz.shape, BF16),
            pltpu.VMEM(wl.shape, BF16),
            pltpu.VMEM((5, 8, PLANE), F32),
            pltpu.VMEM((5, 8, 128), F32),
            pltpu.VMEM((fields, 256, 128), F32),
            pltpu.VMEM((fields, 256, 128), F32),
            pltpu.VMEM((8, fields, 32, 128), F32),
            pltpu.VMEM((8, fields, 32, 128), F32),
            pltpu.VMEM((fields, 256, 128), F32),
            pltpu.VMEM((fields, 256, 128), F32),
            pltpu.VMEM((5, 8, PLANE), F32),
            pltpu.VMEM((5, 8, PLANE), F32),
            pltpu.VMEM((NG, 512), F32),
            dma((5,)),
            pltpu.SemaphoreType.REGULAR,
            dma((5,)),
            dma((5,)),
            dma((3,)),
            dma((5,)),
            dma((len(RUNS), 8)),
            dma((len(RUNS), 8)),
            dma((len(RUNS), 8)),
            dma((len(RUNS), 8)),
            dma((4,)),
            dma((5,)),
        ],
        compiler_params=pltpu.CompilerParams(
            collective_id=0, has_side_effects=True, vmem_limit_bytes=24 * 1024 * 1024
        ),
        cost_estimate=pl.CostEstimate(flops=500_000_000, bytes_accessed=1 << 20, transcendentals=0),
    )(held(orbitals.reshape(16, PLANE)), counts, held(partners), held(jnp.asarray(wz)), held(jnp.asarray(wl)))
    return applied.reshape(1, 16, PLANE)


def solution(mesh):
    in_specs = (P("band", "grid", None), P("band"), P("band", None))
    out_specs = P("band", "grid", None)
    return jax.shard_map(shards, mesh=mesh, in_specs=in_specs, out_specs=out_specs, check_vma=False)
```

time: 55.1 us -> 48.1 us (0.87); the launches traced: 54.1 us -> 48 us
  local copies, waits for them, and re-layouts: 4.16 us -> 0.71 us
  Pallas kernels: 49.3 us -> 46.6 us
    unnamed x9 -> x1, local copies, waits for them, and re-layouts: 4.16 us -> 0.71 us
    pallas_call x1, Pallas kernels: 49.3 us -> 46.6 us  [shards(): pl.pallas_call(kernel, out_shape=jax.ShapeDtypeStruct((16, PLANE), F32),...]
where the time goes in v1:
time: 48.1 us; the launch traced here: 48 us
  Pallas kernels  46.6 us (97%)
  local copies, waits for them, and re-layouts  0.71 us (1%)
  between operations  0.66 us (1%)
    pallas_call x1, Pallas kernels, shards(): pl.pallas_call(kernel, out_shape=jax.ShapeDtypeStruct((16, PLANE), F32),...  46.6 us

profile of v1, /device:TPU:1, one launch (start us, length us, event | category | flops | bytes accessed | tf_op | source)
XLA Modules:
  0.0 48.0 jit_solution(8538771964850989447)
XLA Ops:
  0.7 46.6 %shard_map.55 = f32[16,4096]{1,0:T(8,128)S(1)} custom-call(f32[16,4096]{1,0:T(8,128)} %bitcast.3, s32[1]{0:T(128)S(6)} %copy.7.counts_in, s32[1,3]{1,0:T(1,128)} %partners_in.1, bf16[2,256,256]{2,1,0:T(8,128)(2,1)} %constant.4.clone.wz_in, bf16[4,64,192]{2,1,0:T(8,128)(2,1)} %constant.5.clone.wl_in), custom_call_target="tpu_custom_call" | custom-call | flops 500000000 | bytes 1048576 | tf_op jit(solution)/shard_map/pallas_call | solution.py:344
  47.3 0.7 %copy.8 = f32[1,16,4096]{2,1,0:T(8,128)} copy(f32[1,16,4096]{2,1,0:T(8,128)S(1)} %bitcast.2) | data formatting | bytes 524288

commit v2 on v1

--- a/solution.py
+++ b/solution.py
@@ -15,9 +15,9 @@
 NG = 64
 PLANE = NG * NG
 B, C, D, E, F = range(5)
-PAIRS = ((D, E, 1), (C, F, 3), (C, D, 1), (C, E, 2), (B, D, 2), (B, E, 3))
-RUNS = ((0, 1), (1, 2), (3, 2), (5, 1))
-PLAN = (("f", 0), ("f", 1), ("f", 2), ("x", 0), ("f", 3), ("x", 1), ("x", 2), ("x", 3), ("i", 0), ("i", 1), ("i", 2), ("i", 3))
+PAIRS = ((D, E, 1), (C, E, 2), (C, D, 1), (C, F, 3), (B, D, 2), (B, E, 3))
+RUNS = ((0, 1), (1, 3), (4, 2))
+PLAN = (("f", 0), ("f", 1), ("f", 2), ("x", 1), ("x", 2), ("x", 0), ("i", 1), ("i", 2), ("i", 0))
 
 
 def basis():
@@ -265,7 +265,7 @@
         return remote(acc.at[slot], ret.at[to], r_send.at[n], r_recv.at[to], device)
 
     gives = {
-        B: give(B, 1 + h, 0, at(-1, 0)),
+        B: give(B, 1, 0, at(-1, h)),
         C: give(C, 3, 1, at(-1, h)),
         F: give(F, 4, 2, at(1, h)),
     }
@@ -309,23 +309,14 @@
 
     returned(4)
     returned(3)
-    acc[D] = acc[D] + ret[4]
+    returned(1)
+    acc[D] = acc[D] + ret[4] + ret[1]
     acc[E] = acc[E] + ret[3]
     swap.start()
 
-    @pl.when(h == 0)
-    def _():
-        returned(1)
-        returned(2)
-        out_ref[0:8, :] = acc[D] + ret[1]
-        returned(0)
-        out_ref[8:16, :] = ret[0] + ret[2]
-
-    @pl.when(h == 1)
-    def _():
-        out_ref[8:16, :] = acc[E]
-        returned(0)
-        out_ref[0:8, :] = ret[0]
+    out_ref[rows(h), :] = acc[D + h]
+    returned(0)
+    out_ref[rows(1 - h), :] = ret[0]
 
     for copy in sent + list(gives.values()) + [swap]:
         copy.wait_send()

time: 48.1 us -> 46.4 us (0.965)
  Pallas kernels: 46.6 us -> 44.5 us
    pallas_call x1, Pallas kernels: 46.6 us -> 44.5 us  [shards(): pl.pallas_call(kernel, out_shape=jax.ShapeDtypeStruct((16, PLANE), F32),...]
where the time goes in v2:
time: 46.4 us; the launch traced here: 45.9 us
  Pallas kernels  44.5 us (96%)
  local copies, waits for them, and re-layouts  0.71 us (2%)
  between operations  0.66 us (1%)
    pallas_call x1, Pallas kernels, shards(): pl.pallas_call(kernel, out_shape=jax.ShapeDtypeStruct((16, PLANE), F32),...  44.5 us

profile of v2, /device:TPU:1, one launch (start us, length us, event | category | flops | bytes accessed | tf_op | source)
XLA Modules:
  0.0 45.9 jit_solution(8444961121145524526)
XLA Ops:
  0.7 44.5 %shard_map.55 = f32[16,4096]{1,0:T(8,128)S(1)} custom-call(f32[16,4096]{1,0:T(8,128)} %bitcast.3, s32[1]{0:T(128)S(6)} %copy.7.counts_in, s32[1,3]{1,0:T(1,128)} %partners_in.1, bf16[2,256,256]{2,1,0:T(8,128)(2,1)} %constant.4.clone.wz_in, bf16[4,64,192]{2,1,0:T(8,128)(2,1)} %constant.5.clone.wl_in), custom_call_target="tpu_custom_call" | custom-call | flops 500000000 | bytes 1048576 | tf_op jit(solution)/shard_map/pallas_call | solution.py:335
  45.2 0.7 %copy.8 = f32[1,16,4096]{2,1,0:T(8,128)} copy(f32[1,16,4096]{2,1,0:T(8,128)S(1)} %bitcast.2) | data formatting | bytes 524288

commit v3 on v2

--- a/solution.py
+++ b/solution.py
@@ -315,11 +315,10 @@
     swap.start()
 
     out_ref[rows(h), :] = acc[D + h]
+    for copy in sent + list(gives.values()) + [swap]:
+        copy.wait_send()
     returned(0)
     out_ref[rows(1 - h), :] = ret[0]
-
-    for copy in sent + list(gives.values()) + [swap]:
-        copy.wait_send()
 
 
 def shards(orbitals, counts, partners):

time: 46.4 us -> 46.3 us (level)
  no operation moved by 1% of the time
where the time goes in v3:
time: 46.3 us; the launch traced here: 45.8 us
  Pallas kernels  44.4 us (96%)
  local copies, waits for them, and re-layouts  0.71 us (2%)
  between operations  0.66 us (1%)
    pallas_call x1, Pallas kernels, shards(): pl.pallas_call(kernel, out_shape=jax.ShapeDtypeStruct((16, PLANE), F32),...  44.4 us

profile of v3, /device:TPU:1, one launch (start us, length us, event | category | flops | bytes accessed | tf_op | source)
XLA Modules:
  0.0 45.8 jit_solution(10726831617157155018)
XLA Ops:
  0.7 44.4 %shard_map.55 = f32[16,4096]{1,0:T(8,128)S(1)} custom-call(f32[16,4096]{1,0:T(8,128)} %bitcast.3, s32[1]{0:T(128)S(6)} %copy.7.counts_in, s32[1,3]{1,0:T(1,128)} %partners_in.1, bf16[2,256,256]{2,1,0:T(8,128)(2,1)} %constant.4.clone.wz_in, bf16[4,64,192]{2,1,0:T(8,128)(2,1)} %constant.5.clone.wl_in), custom_call_target="tpu_custom_call" | custom-call | flops 500000000 | bytes 1048576 | tf_op jit(solution)/shard_map/pallas_call | solution.py:334
  45.1 0.7 %copy.8 = f32[1,16,4096]{2,1,0:T(8,128)} copy(f32[1,16,4096]{2,1,0:T(8,128)S(1)} %bitcast.2) | data formatting | bytes 524288

commit v4 on v3

--- a/solution.py
+++ b/solution.py
@@ -102,7 +102,7 @@
 
 def kernel(
     orb, counts_in, partners_in, wz_in, wl_in, out_ref,
-    counts, partners, wz_ref, wl_ref, band, listed, s1, s2, got, back, s3, s4, acc, ret, lam,
+    counts, partners, wz_ref, wl_ref, band, spare, listed, s1, s2, got, back, s3, s4, acc, ret, lam,
     local_sem, hello, f_send, f_recv, a_send, a_recv, t1_send, t1_recv, t2_send, t2_recv, r_send, r_recv,
 ):
     m = lax.axis_index("band")
@@ -134,7 +134,7 @@
         pltpu.make_async_copy(src, dst, local_sem.at[n])
         for n, (src, dst) in enumerate(
             (
-                (counts_in, counts), (partners_in, partners), (mine, band.at[D + h]),
+                (mine, band.at[D + h]), (rest, spare), (counts_in, counts), (partners_in, partners),
                 (wz_in, wz_ref), (wl_in, wl_ref),
             )
         )
@@ -142,6 +142,8 @@
     for copy in local:
         copy.start()
 
+    local[1].wait()
+    local[0].wait()
     pl.semaphore_wait(barrier, 6)
 
     def fetch(src, slot, n, device):
@@ -154,16 +156,16 @@
         return remote(listed.at[D + h], listed.at[slot], a_send.at[n], a_recv.at[slot], device)
 
     sent = [
-        fetch(rest, D + h, 0, at(0, 1 - h)),
-        fetch(mine, B + h, 1, at(1, h)),
+        fetch(spare, D + h, 0, at(0, 1 - h)),
+        fetch(band.at[D + h], B + h, 1, at(1, h)),
     ]
     for copy in sent:
         copy.start()
     for hh in range(2):
         pl.semaphore_signal(hello, inc=1, device_id=at(1, hh), device_id_type=MESH)
 
-    local[0].wait()
-    local[1].wait()
+    local[2].wait()
+    local[3].wait()
     row = lax.broadcasted_iota(jnp.int32, (8, 128), 0)
     tile = jnp.zeros((8, 128), F32)
     for d in range(1, 4):
@@ -187,7 +189,7 @@
         some = total > 0
         lam[:, 128 * i : 128 * (i + 1)] = jnp.where(some, F32(4 * math.pi) / jnp.where(some, total, 1.0), 0.0)
 
-    for copy in local[2:]:
+    for copy in local[4:]:
         copy.wait()
     fetched(E - h)
     tell(E - h, 0, at(0, 1 - h)).wait_recv()
@@ -342,6 +344,7 @@
             pltpu.VMEM(wz.shape, BF16),
             pltpu.VMEM(wl.shape, BF16),
             pltpu.VMEM((5, 8, PLANE), F32),
+            pltpu.VMEM((8, PLANE), F32),
             pltpu.VMEM((5, 8, 128), F32),
             pltpu.VMEM((fields, 256, 128), F32),
             pltpu.VMEM((fields, 256, 128), F32),
@@ -352,7 +355,7 @@
             pltpu.VMEM((5, 8, PLANE), F32),
             pltpu.VMEM((5, 8, PLANE), F32),
             pltpu.VMEM((NG, 512), F32),
-            dma((5,)),
+            dma((6,)),
             pltpu.SemaphoreType.REGULAR,
             dma((5,)),
             dma((5,)),

time: 46.3 us -> 46.3 us (level)
  no operation moved by 1% of the time
where the time goes in v4:
time: 46.3 us; the launch traced here: 45.6 us
  Pallas kernels  44.3 us (96%)
  local copies, waits for them, and re-layouts  0.71 us (2%)
  between operations  0.66 us (1%)
    pallas_call x1, Pallas kernels, shards(): pl.pallas_call(kernel, out_shape=jax.ShapeDtypeStruct((16, PLANE), F32),...  44.3 us

profile of v4, /device:TPU:1, one launch (start us, length us, event | category | flops | bytes accessed | tf_op | source)
XLA Modules:
  0.0 45.6 jit_solution(17479134662969778243)
XLA Ops:
  0.7 44.3 %shard_map.55 = f32[16,4096]{1,0:T(8,128)S(1)} custom-call(f32[16,4096]{1,0:T(8,128)} %bitcast.3, s32[1]{0:T(128)S(6)} %copy.7.counts_in, s32[1,3]{1,0:T(1,128)} %partners_in.1, bf16[2,256,256]{2,1,0:T(8,128)(2,1)} %constant.4.clone.wz_in, bf16[4,64,192]{2,1,0:T(8,128)(2,1)} %constant.5.clone.wl_in), custom_call_target="tpu_custom_call" | custom-call | flops 500000000 | bytes 1048576 | tf_op jit(solution)/shard_map/pallas_call | solution.py:336
  44.9 0.7 %copy.8 = f32[1,16,4096]{2,1,0:T(8,128)} copy(f32[1,16,4096]{2,1,0:T(8,128)S(1)} %bitcast.2) | data formatting | bytes 524288

commit v5 on v4

--- a/solution.py
+++ b/solution.py
@@ -310,10 +310,11 @@
         give(B, slot, 0, at(-1, 0)).wait_recv()
 
     returned(4)
+    acc[D] = acc[D] + ret[4]
     returned(3)
+    acc[E] = acc[E] + ret[3]
     returned(1)
-    acc[D] = acc[D] + ret[4] + ret[1]
-    acc[E] = acc[E] + ret[3]
+    acc[D] = acc[D] + ret[1]
     swap.start()
 
     out_ref[rows(h), :] = acc[D + h]

time: 46.3 us -> 46.4 us (level)
  no operation moved by 1% of the time
where the time goes in v5:
time: 46.4 us; the launch traced here: 45.6 us
  Pallas kernels  44.3 us (95%)
  local copies, waits for them, and re-layouts  0.71 us (2%)
  between operations  0.66 us (1%)
    pallas_call x1, Pallas kernels, shards(): pl.pallas_call(kernel, out_shape=jax.ShapeDtypeStruct((16, PLANE), F32),...  44.3 us

profile of v5, /device:TPU:1, one launch (start us, length us, event | category | flops | bytes accessed | tf_op | source)
XLA Modules:
  0.0 45.6 jit_solution(15360948406455751416)
XLA Ops:
  0.7 44.3 %shard_map.55 = f32[16,4096]{1,0:T(8,128)S(1)} custom-call(f32[16,4096]{1,0:T(8,128)} %bitcast.3, s32[1]{0:T(128)S(6)} %copy.7.counts_in, s32[1,3]{1,0:T(1,128)} %partners_in.1, bf16[2,256,256]{2,1,0:T(8,128)(2,1)} %constant.4.clone.wz_in, bf16[4,64,192]{2,1,0:T(8,128)(2,1)} %constant.5.clone.wl_in), custom_call_target="tpu_custom_call" | custom-call | flops 500000000 | bytes 1048576 | tf_op jit(solution)/shard_map/pallas_call | solution.py:337
  44.9 0.7 %copy.8 = f32[1,16,4096]{2,1,0:T(8,128)} copy(f32[1,16,4096]{2,1,0:T(8,128)S(1)} %bitcast.2) | data formatting | bytes 524288
